TPU v7x, 32 devices: a whole 2x2x4 slice. The times are simulated.
32 devices in a mesh: row: 4 (over z), col: 8 (over y, x, core).
Axes of the slice: x: 2, y: 2, z: 4, core: 2. Of those that a mesh axis runs over, the one named last changes fastest.
Arguments:
- tiles: bfloat16 [4, 8, 96, 256, 256], P('row', 'col'), may hold values from 0 to 1
- tile_coord: int32 [4, 8, 96, 2], P('row', 'col'), may hold values from 0 to 15, as said below
- tile_count: int32 [4, 8], P('row', 'col'), may hold values from 0 to 96, as said below
- factors: bfloat16 [16384, 256], P(('row', 'col')), may hold values from -0.09375 to 0.09375
- owner: int32 [16384], P(('row', 'col')), may hold values from 0 to 16383, as said below
- gram_inverse: float32 [256, 256], replicated, as said below
Outputs:
- solution: float32 [16384, 256], P(('row', 'col'))
Inputs may be any that keep to these rules, and one draw needn't show every extreme that they name: `tile_coord`: slots below a block's count hold distinct tile positions with r * 16 + i <= c * 8 + j; later slots are unused. Some block has all 96 slots used; blocks below the diagonal have none. `tile_count`: at most 96, reached in every draw. `owner`: A permutation of 0 to 16383; each block of 512 consecutive words has exactly 16 words whose value divided by 512 is d, for every device d. `gram_inverse`: Symmetric.
All inputs are finite; a program needn't handle non-finite values.
Results may differ from a plain program's by a relative error of at most 0.0003.
Values may be sent and summed in bfloat16 or wider, within the bound.
A program may use at most 128 MiB of HBM per device.

v0:
```python
import math

import jax
import jax.numpy as jnp
from jax import lax
from jax.sharding import PartitionSpec as P


def spread(value, axis, root):
    mine = lax.axis_index(axis) == root
    return lax.psum(jnp.where(mine, value, jnp.zeros_like(value)), axis)


def tile_pass(slabs, coords, first_live, last_live, row_tiles, col_tiles, row_base, col_base):
    slot_total = slabs.shape[0]
    tiles_per_block = math.gcd(16, slot_total)
    tile_dim = slabs.shape[-1]
    rank_dim = row_tiles.shape[-1]
    row_span = row_tiles.shape[0]
    col_span = col_tiles.shape[0]
    first_live = jnp.maximum(first_live, 0)
    last_live = jnp.maximum(last_live, first_live)
    init_sums = (
        jnp.zeros((row_span, tile_dim * rank_dim), jnp.float32),
        jnp.zeros((col_span, tile_dim * rank_dim), jnp.float32),
    )
    row_ids = jnp.arange(row_span, dtype=jnp.int32)[:, None]
    col_ids = jnp.arange(col_span, dtype=jnp.int32)[:, None]

    def block_step(block_idx, sum_pair):
        first_slot = block_idx * tiles_per_block
        tile_block = lax.dynamic_slice_in_dim(slabs, first_slot, tiles_per_block, 0)
        tile_where = lax.dynamic_slice_in_dim(coords, first_slot, tiles_per_block, 0)
        slot_ids = first_slot + jnp.arange(tiles_per_block, dtype=jnp.int32)
        is_valid = (slot_ids >= first_live) & (slot_ids < last_live)
        tile_row = tile_where[:, 0]
        tile_col = tile_where[:, 1]
        is_upper = is_valid & (row_base + tile_row < col_base + tile_col)
        row_sums, col_sums = sum_pair
        right_tiles = jnp.take(col_tiles, tile_col, axis=0)
        row_terms = jnp.einsum(
            "sij,sjk->sik", tile_block, right_tiles, preferred_element_type=jnp.float32
        )
        left_tiles = jnp.take(row_tiles, tile_row, axis=0)
        col_terms = jnp.einsum(
            "sij,sik->sjk", tile_block, left_tiles, preferred_element_type=jnp.float32
        )
        row_select = ((row_ids == tile_row[None, :]) & is_valid[None, :]).astype(jnp.float32)
        col_select = ((col_ids == tile_col[None, :]) & is_upper[None, :]).astype(jnp.float32)
        row_sums = row_sums + jnp.dot(
            row_select, row_terms.reshape(tiles_per_block, -1), precision=lax.Precision.HIGHEST
        )
        col_sums = col_sums + jnp.dot(
            col_select, col_terms.reshape(tiles_per_block, -1), precision=lax.Precision.HIGHEST
        )
        return (row_sums, col_sums)

    first_block = first_live // tiles_per_block
    block_total = (last_live + tiles_per_block - 1) // tiles_per_block
    row_sums, col_sums = lax.fori_loop(first_block, block_total, block_step, init_sums)
    return (
        row_sums.reshape(row_span * tile_dim, rank_dim),
        col_sums.reshape(col_span * tile_dim, rank_dim),
    )


def pack_rows(values, targets, own_rows, devices):
    dest_ids = targets // own_rows
    sort_order = jnp.argsort(dest_ids, stable=True)
    moved = jnp.take(values, sort_order, axis=0).reshape(devices, -1, values.shape[1])
    slot_ids = jnp.take(targets % own_rows, sort_order).reshape(devices, -1)
    return (moved, slot_ids)


def per_device(tiles, tile_coord, tile_count, factors, owner, gram_inverse):
    n_row = lax.axis_size("row")
    n_col = lax.axis_size("col")
    devices = n_row * n_col
    row_at = lax.axis_index("row")
    col_at = lax.axis_index("col")
    own_rows, rank_dim = factors.shape
    row_panel, row_owner = (
        lax.all_gather(factors, "col", axis=0, tiled=True),
        lax.all_gather(owner, "col", axis=0, tiled=True),
    )
    ratio = n_col // n_row
    col_words = own_rows * n_row
    offset = col_at % ratio * col_words
    local_panel = lax.dynamic_slice_in_dim(row_panel, offset, col_words, 0)
    local_owner = lax.dynamic_slice_in_dim(row_owner, offset, col_words, 0)
    col_panel, col_owner = (
        spread(local_panel, "row", col_at // ratio),
        spread(local_owner, "row", col_at // ratio),
    )
    tile_dim = tiles.shape[-1]
    row_tiles = row_panel.reshape(-1, tile_dim, rank_dim)
    col_tiles = col_panel.reshape(-1, tile_dim, rank_dim)
    slabs = tiles[0, 0]
    coords = tile_coord[0, 0]
    live_count = tile_count[0, 0]
    row_base = row_at * row_tiles.shape[0]
    col_base = col_at * col_tiles.shape[0]
    row_parts, col_parts = tile_pass(
        slabs, coords, 0, live_count, row_tiles, col_tiles, row_base, col_base
    )
    row_piece = lax.psum_scatter(row_parts, "col", scatter_dimension=0, tiled=True)
    col_piece = lax.psum_scatter(col_parts, "row", scatter_dimension=0, tiled=True)
    piece_owner = lax.dynamic_slice_in_dim(col_owner, row_at * own_rows, own_rows, 0)
    values = jnp.concatenate([row_piece, col_piece], axis=0)
    targets = jnp.concatenate([owner, piece_owner], axis=0)
    moved, slot_ids = pack_rows(values, targets, own_rows, devices)
    got_rows, got_slots = (
        lax.all_to_all(moved, ("row", "col"), split_axis=0, concat_axis=0, tiled=True),
        lax.all_to_all(slot_ids, ("row", "col"), split_axis=0, concat_axis=0, tiled=True),
    )
    placed = (
        jnp.zeros((own_rows, rank_dim), jnp.float32)
        .at[got_slots.reshape(-1)]
        .add(got_rows.reshape(-1, rank_dim))
    )
    return jnp.dot(placed, gram_inverse, precision=lax.Precision.HIGHEST)


def solution(mesh):
    in_specs = (
        P("row", "col", None, None, None),
        P("row", "col", None, None),
        P("row", "col"),
        P(("row", "col"), None),
        P(("row", "col")),
        P(),
    )
    out_specs = P(("row", "col"), None)
    return jax.shard_map(
        per_device, mesh=mesh, in_specs=in_specs, out_specs=out_specs, check_vma=False
    )
```

profile of v0, /device:TPU:0, one launch (start us, length us, event | category | flops | bytes accessed | tf_op | source)
XLA Modules:
  0.0 384.8 jit_solution(11135530983871108879)
XLA Ops:
  7.3 32.5 %all-gather.3.cloned.1.call-done = bf16[4096,256]{1,0:T(8,128)(2,1)} async-done(((bf16[512,256]{1,0:T(8,128)(2,1)}), bf16[4096,256]{1,0:T(8,128)(2,1)}) %all-gather.3.cloned.1.call-update) | async-done | bytes 2097168 | tf_op jit(solution)/shard_map/all_gather | solution.py:83
  39.9 2.4 dynamic-slice_select_fusion
  43.0 51.3 %all-reduce.2.cloned.1.call-done = bf16[8,256,256]{2,1,0:T(8,128)(2,1)} async-done(((bf16[8,256,256]{2,1,0:T(8,128)(2,1)}), bf16[8,256,256]{2,1,0:T(8,128)(2,1)}) %all-reduce.2.cloned.1.call-update) | async-done | bytes 1048592 | tf_op jit(solution)/shard_map/psum | solution.py:11
  98.1 68.2 %while.13 = (s32[]{:T(128)}, f32[16,65536]{1,0:T(8,128)}, f32[8,65536]{1,0:T(8,128)}, s32[]{:T(128)}, s32[96,2]{0,1:T(2,128)S(1)}, /*index=5*/s32[]{:T(128)}, bf...) while((s32[]{:T(128)}, f32[16,65536]{1,0:T(8,128)}, ...), condition=%wide.region_4.5_spmd.clone, body=%wide.region_3.4_spmd.clone.sunk | while | flops 1379405056 | bytes 113256136 | solution.py:60
  101.3 2.4 copy.15
  103.8 4.2 %convolution_add_fusion.4 = f32[16,65536]{1,0:T(8,128)S(1)} fusion(f32[16,65536]{1,0:T(8,128)S(1)} %copy-done.1, f32[16,65536]{1,0:T(8,128)S(1)} %bitcast.54, s32[16]{0:T(128)S(1)} %get-tuple-element.222, pred[16]{0:T(512)(128)(4,1)S(1)} %get-tuple-element.223), kind=kOutput, calls=%fused_computation.7.clone.1 | convolution fusion | flops 202375680 | bytes 12582992 | tf_op jit(solution)/shard_map/while/body/dot_general | solution.py:50
  112.2 2.4 fusion.56
  114.6 2.4 copy.16
  117.1 2.4 convolution_add_fusion.5
  124.0 2.4 copy.15
  126.5 4.2 %convolution_add_fusion.4 = f32[16,65536]{1,0:T(8,128)S(1)} fusion(f32[16,65536]{1,0:T(8,128)S(1)} %copy-done.1, f32[16,65536]{1,0:T(8,128)S(1)} %bitcast.54, s32[16]{0:T(128)S(1)} %get-tuple-element.222, pred[16]{0:T(512)(128)(4,1)S(1)} %get-tuple-element.223), kind=kOutput, calls=%fused_computation.7.clone.1 | convolution fusion | flops 202375680 | bytes 12582992 | tf_op jit(solution)/shard_map/while/body/dot_general | solution.py:50
  134.9 2.4 fusion.56
  137.3 2.4 copy.16
  139.8 2.4 convolution_add_fusion.5
  146.8 2.4 copy.15
  149.2 4.2 %convolution_add_fusion.4 = f32[16,65536]{1,0:T(8,128)S(1)} fusion(f32[16,65536]{1,0:T(8,128)S(1)} %copy-done.1, f32[16,65536]{1,0:T(8,128)S(1)} %bitcast.54, s32[16]{0:T(128)S(1)} %get-tuple-element.222, pred[16]{0:T(512)(128)(4,1)S(1)} %get-tuple-element.223), kind=kOutput, calls=%fused_computation.7.clone.1 | convolution fusion | flops 202375680 | bytes 12582992 | tf_op jit(solution)/shard_map/while/body/dot_general | solution.py:50
  157.6 2.4 fusion.56
  160.1 2.4 copy.16
  162.5 2.4 convolution_add_fusion.5
  166.3 3.3 reshape.127
  169.6 3.9 %reshape.126 = f32[4096,256]{1,0:T(8,128)} reshape(f32[16,65536]{1,0:T(8,128)} %get-tuple-element.76) | data formatting | bytes 8388608 | tf_op jit(solution)/shard_map/reshape | solution.py:62
  174.2 77.0 %all-gather = s32[8,1,512]{2,1,0:T(1,128)S(1)} all-gather(s32[1,1,512]{2,1,0:T(1,128)S(1)} %bitcast.65), channel_id=1, replica_groups=mesh['row'=4,'col'=8] {'col'}, dimensions={0}, use_global_device_ids=true | all-gather | bytes 18432 | tf_op jit(solution)/shard_map/all_gather | solution.py:84
  251.3 6.5 %psum.14 = s32[2048]{0:T(1024)S(1)} all-reduce(s32[2048]{0:T(1024)S(1)} %dynamic-slice_select_fusion.1), channel_id=1, replica_groups=mesh['row'=4,'col'=8] {'row'}, use_global_device_ids=true, to_apply=%region_0.1 | all-reduce | flops 2048 | bytes 16384 | tf_op jit(solution)/shard_map/psum | solution.py:11
  257.9 4.4 %sort.17 = (s32[1024]{0:T(1024)}, s32[1024]{0:T(1024)S(1)}) sort(s32[1024]{0:T(1024)S(1)} %get-tuple-element.138, s32[1024]{0:T(1024)S(1)} %iota.19), dimensions={0}, to_apply=%region_1.2 | sort | flops 10240 | bytes 16384 | tf_op jit(solution)/shard_map/jit(argsort)/sort | solution.py:69
  262.2 4.5 %gather_fusion.2 = s32[1024]{0:T(1024)S(1)} fusion(s32[1024]{0:T(1024)S(1)} %get-tuple-element.139, s32[1024]{0:T(1024)S(1)} %fusion.31), kind=kCustom, calls=%fused_computation.2 | custom fusion | bytes 12288 | tf_op jit(solution)/shard_map/jit(_take)/gather | solution.py:71
  267.5 5.4 %all-to-all-start = ((s32[32,1,32]{2,1,0:T(1,128)}), s32[32,1,32]{2,1,0:T(1,128)S(1)}, u32[]{:S(2)}, u32[]{:S(2)}) async-start(s32[32,1,32]{2,1,0:T(1,128)} %select_n.123), calls=%async_computation | async-start | bytes 32768 | tf_op jit(solution)/shard_map/all_to_all | solution.py:114
  273.0 6.9 %reduce-scatter.5.cloned.1.call-done = f32[512,256]{1,0:T(8,128)} async-done(((f32[2048,256]{1,0:T(8,128)}), f32[512,256]{1,0:T(8,128)}) %reduce-scatter.5.cloned.1.call-update) | async-done | bytes 524304 | tf_op jit(solution)/shard_map/reduce_scatter | solution.py:107
  279.9 54.1 %reduce-scatter.3.cloned.1.call-done = f32[512,256]{1,0:T(8,128)} async-done(((f32[4096,256]{1,0:T(8,128)}), f32[512,256]{1,0:T(8,128)}) %reduce-scatter.3.cloned.1.call-update) | async-done | bytes 524304 | tf_op jit(solution)/shard_map/reduce_scatter | solution.py:106
  335.2 3.5 gather_fusion.3
  339.9 4.6 %all-to-all-start.1 = ((f32[32,32,256]{2,1,0:T(8,128)}), f32[32,32,256]{2,1,0:T(8,128)S(1)}, u32[]{:S(2)}, u32[]{:S(2)}) async-start(f32[32,32,256]{2,1,0:T(8,128)} %broadcast_select_fusion), calls=%async_computation.3 | async-start | bytes 2097152 | tf_op jit(solution)/shard_map/all_to_all | solution.py:113
  345.8 24.9 %all-to-all-done.1 = f32[32,32,256]{2,1,0:T(8,128)S(1)} async-done(((f32[32,32,256]{2,1,0:T(8,128)}), f32[32,32,256]{2,1,0:T(8,128)S(1)}, u32[]{:S(2)}, u32[]{:S(2)}) %all-to-all-start.1) | async-done | bytes 1048608 | tf_op jit(solution)/shard_map/all_to_all | solution.py:113
  370.7 6.2 %scatter_custom_fusion = f32[512,256]{1,0:T(8,128)S(1)} fusion(s32[1024]{0:T(1024)S(1)} %bitcast.66, f32[1024,256]{1,0:T(8,128)S(1)} %bitcast.62, f32[]{:T(128)} %constant.147.clone.1), kind=kCustom, calls=%fused_computation.47 | custom fusion | flops 262144 | bytes 524292 | tf_op jit(solution)/shard_map/scatter-add | solution.py:119
  (82 shorter events, 37.5 us)
Async XLA Ops:
  6.5 370.4 %copy-start = (f32[256,256]{1,0:T(8,128)S(1)}, f32[256,256]{1,0:T(8,128)}, u32[]{:S(2)}) copy-start(f32[256,256]{1,0:T(8,128)} %param.13) | copy-start | bytes 786436
  6.5 33.3 %all-gather.3.cloned.1.call-start = ((), (), s32[]{:S(2)}) async-start(), calls=%async_computation.4 | async-start | bytes 2359296 | tf_op jit(solution)/shard_map/all_gather | solution.py:83
  7.3 87.0 %all-reduce.2.cloned.1.call-start = ((), (), s32[]{:S(2)}) async-start(), calls=%async_computation.5 | async-start | bytes 2097152 | tf_op jit(solution)/shard_map/psum | solution.py:11
  42.3 237.6 %reduce-scatter.5.cloned.1.call-start = ((), (), s32[]{:S(2)}) async-start(), calls=%async_computation.7 | async-start | bytes 2621440 | tf_op jit(solution)/shard_map/reduce_scatter | solution.py:107
  96.5 1.6 copy-start.3
  96.5 1.6 copy-start.6
  101.3 2.5 copy-start.1
  108.0 1.9 copy-start.2
  114.6 2.4 copy-start.4
  119.5 1.4 copy-start.5
  124.0 2.5 copy-start.1
  130.7 1.9 copy-start.2
  137.3 2.4 copy-start.4
  142.2 1.4 copy-start.5
  146.8 2.5 copy-start.1
  153.4 1.9 copy-start.2
  160.1 2.4 copy-start.4
  164.9 1.4 copy-start.5
  169.6 164.4 %reduce-scatter.3.cloned.1.call-start = ((), (), s32[]{:S(2)}) async-start(), calls=%async_computation.6 | async-start | bytes 4718592 | tf_op jit(solution)/shard_map/reduce_scatter | solution.py:106
  173.5 0.7 copy-start.7
  267.5 72.4 %all-to-all-start = ((s32[32,1,32]{2,1,0:T(1,128)}), s32[32,1,32]{2,1,0:T(1,128)S(1)}, u32[]{:S(2)}, u32[]{:S(2)}) async-start(s32[32,1,32]{2,1,0:T(1,128)} %select_n.123), calls=%async_computation | async-start | bytes 32768 | tf_op jit(solution)/shard_map/all_to_all | solution.py:114
  339.9 30.8 %all-to-all-start.1 = ((f32[32,32,256]{2,1,0:T(8,128)}), f32[32,32,256]{2,1,0:T(8,128)S(1)}, u32[]{:S(2)}, u32[]{:S(2)}) async-start(f32[32,32,256]{2,1,0:T(8,128)} %broadcast_select_fusion), calls=%async_computation.3 | async-start | bytes 2097152 | tf_op jit(solution)/shard_map/all_to_all | solution.py:113
Sparse Core Ops, SparseCore 0:
  9.2 30.5 all-gather.2
  42.4 51.8 all-reduce.1
  169.7 110.1 reduce-scatter.4
  283.1 50.8 reduce-scatter.2
where the time goes:
time: 386 us; the launch traced here: 385 us
  waiting for transfers between devices  170 us (44%)
  blocking collectives  83.6 us (22%)
  local copies, waits for them, and re-layouts  54.5 us (14%)
  matrix products  35.6 us (9%)
  other arithmetic  16.2 us (4%)
  between operations  13.9 us (4%)
  starting transfers between devices  10.2 us (3%)
    all_gather x1, blocking collectives, per_device(): lax.all_gather(owner, 'col', axis=0, tiled=True)  77 us
    reduce_scatter x1, waiting for transfers between devices, per_device(): lax.psum_scatter(row_parts, 'col', scatter_dimension=0, tiled=True)  54.1 us
    psum x1, waiting for transfers between devices, spread(): return lax.psum(jnp.where(mine, value, jnp.zeros_like(value)), axis)  51.3 us
    all_gather x1, waiting for transfers between devices, per_device(): lax.all_gather(factors, 'col', axis=0, tiled=True)  32.5 us
    all_to_all x1, waiting for transfers between devices, per_device(): lax.all_to_all(moved, ('row', 'col'), split_axis=0, concat_axis=0, tiled=...  24.9 us
    while x30, local copies, waits for them, and re-layouts  24.4 us
    dot_general x3, matrix products, block_step(): jnp.dot(row_select, row_terms.reshape(tiles_per_block, -1), precision=lax...  12.5 us
  transfers between devices with their start and end apart: 6, of which 5 were waited for; matrix products, arithmetic and copies ran while one was open for 5% of the time, Pallas kernels for 0%

commit v1 on v0

v1 whole, which is shorter than its diff:
```python
import functools

import jax
import jax.numpy as jnp
from jax import lax
from jax.experimental import pallas as pl
from jax.experimental.pallas import tpu as pltpu
from jax.sharding import PartitionSpec as P

MESH = pl.DeviceIdType.MESH
ANY = pl.BlockSpec(memory_space=pl.ANY)
VMEM = pl.BlockSpec(memory_space=pltpu.VMEM)
HIGHEST = lax.Precision.HIGHEST
MIB = 1 << 20


def remote(src, dst, send_sem, recv_sem, device):
    return pltpu.make_async_remote_copy(
        src_ref=src, dst_ref=dst, send_sem=send_sem, recv_sem=recv_sem,
        device_id=device, device_id_type=MESH,
    )


def gather_kernel(n_row, n_col, f_ref, row_ref, col_ref, row_send, fwd_send, pair_send, col_send,
                  row_recv, col_recv, local_sem, diag_sem):
    r = lax.axis_index("row")
    c = lax.axis_index("col")
    ratio = n_col // n_row
    chips = n_col // 2
    k, e = c // 2, c % 2
    partner = c + 1 - 2 * e
    used = k >= r * ratio // 2
    up = c // ratio

    barrier = pltpu.get_barrier_semaphore()
    for j in range(1, n_col):
        pl.semaphore_signal(barrier, inc=1, device_id=(r, lax.rem(c + j, n_col)), device_id_type=MESH)
    for d in range(1, n_row):
        @pl.when(r - d >= 0)
        def _(d=d):
            pl.semaphore_signal(barrier, inc=1, device_id=(r - d, r * ratio + c // n_row), device_id_type=MESH)

    @pl.when(r < up)
    def _():
        for i in range(n_row):
            pl.semaphore_signal(barrier, inc=1, device_id=(up, (c % ratio) * n_row + i), device_id_type=MESH)
    pl.semaphore_wait(barrier, n_col - 1 + r + jnp.where(r < up, n_row, 0))

    def row_copy(j):
        return remote(f_ref, row_ref.at[c], row_send.at[j], row_recv.at[c],
                      (r, 2 * lax.rem(k + j, chips) + e))

    def row_goes(j):
        return lax.rem(k + j, chips) >= r * ratio // 2

    def col_copy(d):
        return remote(f_ref, col_ref.at[c % n_row], col_send.at[d], col_recv.at[c % n_row],
                      (r - d, r * ratio + c // n_row))

    for j in range(1, chips):
        @pl.when(row_goes(j))
        def _(j=j):
            row_copy(j).start()
    for d in range(n_row - 1, 0, -1):
        @pl.when(r - d >= 0)
        def _(d=d):
            col_copy(d).start()

    def source(j):
        return 2 * lax.rem(k - j + chips, chips)

    def forward(j):
        s = source(j) + e
        return remote(row_ref.at[s], row_ref.at[s], fwd_send.at[j], row_recv.at[s], (r, partner))

    def arrival(s):
        return remote(f_ref, row_ref.at[s], row_send.at[0], row_recv.at[s], (r, partner))

    @pl.when(used)
    def _():
        own = pltpu.make_async_copy(f_ref, row_ref.at[c], local_sem)
        own.start()
        pair = remote(f_ref, row_ref.at[c], pair_send, row_recv.at[c], (r, partner))
        pair.start()
        for j in range(1, chips):
            arrival(source(j) + e).wait_recv()
            forward(j).start()
        arrival(partner).wait_recv()
        for j in range(1, chips):
            arrival(source(j) + 1 - e).wait_recv()
        own.wait()
        pair.wait_send()
        for j in range(1, chips):
            forward(j).wait_send()

    @pl.when(r == up)
    def _():
        copies = [
            pltpu.make_async_copy(row_ref.at[(c % ratio) * n_row + i], col_ref.at[i], diag_sem.at[i])
            for i in range(n_row)
        ]
        for copy in copies:
            copy.start()
        for copy in copies:
            copy.wait()

    for j in range(1, chips):
        @pl.when(row_goes(j))
        def _(j=j):
            row_copy(j).wait_send()
    for d in range(n_row - 1, 0, -1):
        @pl.when(r - d >= 0)
        def _(d=d):
            col_copy(d).wait_send()

    @pl.when(r < up)
    def _():
        for i in range(n_row):
            remote(f_ref, col_ref.at[i], col_send.at[0], col_recv.at[i], (r, partner)).wait_recv()


def encode(x):
    most = jnp.max(jnp.abs(x), axis=1, keepdims=True)
    scale = jnp.maximum(most * (1.01 / 32767.0), 1e-30).astype(jnp.bfloat16).astype(jnp.float32)
    coded = jnp.round(x * (1.0 / scale)).astype(jnp.int32).astype(jnp.int16)
    return coded, scale


def split(coded):
    v = coded.astype(jnp.int32)
    high = (v + 128) >> 8
    low = v - (high << 8)
    return (
        (high << 8).astype(jnp.float32).astype(jnp.bfloat16),
        low.astype(jnp.float32).astype(jnp.bfloat16),
    )


def tile_kernel(per_step, coord_ref, meta_ref, tiles_ref, row_ref, col_ref,
                qrow_ref, qcol_ref, srow_ref, scol_ref, row_sum, col_sum):
    step = pl.program_id(0)
    count = meta_ref[0]
    tile_dim = tiles_ref.shape[-1]

    @pl.when(step == 0)
    def _():
        row_sum[...] = jnp.zeros_like(row_sum)
        col_sum[...] = jnp.zeros_like(col_sum)

    for s in range(per_step):
        slot = step * per_step + s

        @pl.when(slot < count)
        def _(s=s, slot=slot):
            i = coord_ref[2 * slot]
            j = coord_ref[2 * slot + 1]
            tile = tiles_ref[s]
            row_sum[i] += jnp.dot(tile, col_ref[j], preferred_element_type=jnp.float32)

            @pl.when(meta_ref[1] + i < meta_ref[2] + j)
            def _():
                col_sum[j] += lax.dot_general(
                    tile, row_ref[i], (((0,), (0,)), ((), ())), preferred_element_type=jnp.float32
                )

    @pl.when(step == pl.num_programs(0) - 1)
    def _():
        eye = (lax.broadcasted_iota(jnp.int32, (tile_dim, tile_dim), 0)
               == lax.broadcasted_iota(jnp.int32, (tile_dim, tile_dim), 1))

        def code(total, coded_ref, scale_ref):
            @pl.loop(0, total.shape[0])
            def _(t):
                coded, scale = encode(total[t])
                coded_ref[t] = coded
                scale_ref[t] = jnp.sum(jnp.where(eye, scale, 0.0), axis=0, keepdims=True)

        code(row_sum, qrow_ref, srow_ref)
        code(col_sum, qcol_ref, scol_ref)


def solve_kernel(n_row, n_col, pad, tile_dim, qrow_ref, qcol_ref, srow_ref, scol_ref, owner_lane, owner_sub, ginv_ref,
                 out_ref, rq, rs, cq, cs, pick, total, qa, meta, ra, rm,
                 row_send, rsc_send, col_send, csc_send, row_recv, rsc_recv, col_recv, csc_recv,
                 a_send, m_send, a_recv, m_recv, local_sem):
    r = lax.axis_index("row")
    c = lax.axis_index("col")
    me = r * n_col + c
    devices = n_row * n_col
    ratio = n_col // n_row
    own, rank = out_ref.shape
    tpd = own // tile_dim
    packed = devices * pad
    up = c // ratio
    used = r <= up

    barrier = pltpu.get_barrier_semaphore()

    @pl.loop(1, devices)
    def _(d):
        to = lax.rem(me + d, devices)
        pl.semaphore_signal(barrier, inc=1, device_id=(to // n_col, to % n_col), device_id_type=MESH)
    pl.semaphore_wait(barrier, devices - 1)

    def row_copies(j):
        to = lax.rem(c + j, n_col)
        return (
            remote(qrow_ref.at[to], rq.at[c], row_send.at[j], row_recv.at[c], (r, to)),
            remote(srow_ref.at[pl.ds(to * tpd, tpd)], rs.at[pl.ds(c * tpd, tpd)],
                   rsc_send.at[j], rsc_recv.at[c], (r, to)),
        )

    def col_copies(i):
        to = (up, (c % ratio) * n_row + i)
        return (
            remote(qcol_ref.at[i], cq.at[r], col_send.at[i], col_recv.at[r], to),
            remote(scol_ref.at[pl.ds(i * tpd, tpd)], cs.at[pl.ds(r * tpd, tpd)],
                   csc_send.at[i], csc_recv.at[r], to),
        )

    def col_here(i):
        return (
            pltpu.make_async_copy(qcol_ref.at[i], cq.at[r], col_recv.at[r]),
            pltpu.make_async_copy(scol_ref.at[pl.ds(i * tpd, tpd)], cs.at[pl.ds(r * tpd, tpd)], csc_recv.at[r]),
        )

    def col_mine(i):
        return (r == up) & ((c % ratio) * n_row + i == c)

    row_here = (
        pltpu.make_async_copy(qrow_ref.at[c], rq.at[c], row_recv.at[c]),
        pltpu.make_async_copy(srow_ref.at[pl.ds(c * tpd, tpd)], rs.at[pl.ds(c * tpd, tpd)], rsc_recv.at[c]),
    )

    @pl.when(used)
    def _():
        for i in range(n_row):
            @pl.when(jnp.logical_not(col_mine(i)))
            def _(i=i):
                for copy in col_copies(i):
                    copy.start()

            @pl.when(col_mine(i))
            def _(i=i):
                for copy in col_here(i):
                    copy.start()
        for j in range(1, n_col):
            for copy in row_copies(j):
                copy.start()
        for copy in row_here:
            copy.start()

    ow = owner_lane[...]
    dest = ow // own
    slot = (ow - dest * own).astype(jnp.float32)
    same = (owner_sub[...] // own == dest) & (
        lax.broadcasted_iota(jnp.int32, (own, own), 0) < lax.broadcasted_iota(jnp.int32, (own, own), 1))
    place = dest * pad + jnp.sum(same.astype(jnp.int32), axis=0, keepdims=True)
    chosen = lax.broadcasted_iota(jnp.int32, (packed, own), 0) == place
    pick[...] = chosen.astype(jnp.float32)
    slot_sub = jnp.sum(jnp.where(chosen, slot, 0.0), axis=1, keepdims=True)
    total[...] = jnp.zeros_like(total)

    def add(coded_ref, scales_ref, s):
        for t in range(tpd):
            words = pl.ds(t * tile_dim, tile_dim)
            scaled = (pick[:, words] * scales_ref[s * tpd + t]).astype(jnp.bfloat16)
            high, low = split(coded_ref[s, words, :])
            total[...] += (jnp.dot(scaled, high, preferred_element_type=jnp.float32)
                           + jnp.dot(scaled, low, preferred_element_type=jnp.float32))

    def row_arrival(s):
        remote(qrow_ref.at[0], rq.at[s], row_send.at[0], row_recv.at[s], (r, s)).wait_recv()
        remote(srow_ref.at[pl.ds(0, tpd)], rs.at[pl.ds(s * tpd, tpd)], rsc_send.at[0], rsc_recv.at[s],
               (r, s)).wait_recv()

    def col_arrival(s):
        remote(qcol_ref.at[0], cq.at[s], col_send.at[0], col_recv.at[s], (s, c)).wait_recv()
        remote(scol_ref.at[pl.ds(0, tpd)], cs.at[pl.ds(s * tpd, tpd)], csc_send.at[0], csc_recv.at[s],
               (s, c)).wait_recv()

    @pl.when(used)
    def _():
        for copy in row_here:
            copy.wait()
        add(rq, rs, c)

    for d in range(n_row):
        @pl.when(r - d >= 0)
        def _(d=d):
            if d == 0:
                mine = c == (r * ratio + c // n_row)

                @pl.when(mine)
                def _():
                    for copy in col_here(c % n_row):
                        copy.wait()

                @pl.when(jnp.logical_not(mine))
                def _():
                    col_arrival(r)
            else:
                col_arrival(r - d)
            add(cq, cs, r - d)

    for j in range(1, n_col):
        s = lax.rem(c - j + n_col, n_col)

        @pl.when(s >= r * ratio)
        def _(s=s):
            row_arrival(s)
            add(rq, rs, s)

    coded, scale = encode(total[...])
    qa[...] = coded.reshape(devices, pad, rank)
    lane = lax.broadcasted_iota(jnp.int32, (packed, 128), 1)
    within = lax.broadcasted_iota(jnp.int32, (packed, 128), 0) % pad
    spread = jnp.where(lane == within, scale, 0.0) + jnp.where(lane == within + 64, slot_sub, 0.0)
    meta[...] = jnp.broadcast_to(
        jnp.sum(spread.reshape(devices, pad, 128), axis=1, keepdims=True), meta.shape)

    def out_copies(d):
        to = lax.rem(me + d, devices)
        device = (to // n_col, to % n_col)
        return (
            remote(qa.at[to], ra.at[me], a_send.at[d], a_recv.at[me], device),
            remote(meta.at[to], rm.at[me], m_send.at[d], m_recv.at[me], device),
        )

    @pl.loop(1, devices)
    def _(d):
        for copy in out_copies(d):
            copy.start()
    here = (
        pltpu.make_async_copy(qa.at[me], ra.at[me], local_sem.at[0]),
        pltpu.make_async_copy(meta.at[me], rm.at[me], local_sem.at[1]),
    )
    for copy in here:
        copy.start()
    for copy in here:
        copy.wait()

    @pl.when(used)
    def _():
        for i in range(n_row):
            @pl.when(jnp.logical_not(col_mine(i)))
            def _(i=i):
                for copy in col_copies(i):
                    copy.wait_send()
        for j in range(1, n_col):
            for copy in row_copies(j):
                copy.wait_send()

    @pl.loop(1, devices)
    def _(d):
        s = lax.rem(me - d + devices, devices)
        device = (s // n_col, s % n_col)
        remote(qa.at[0], ra.at[s], a_send.at[0], a_recv.at[s], device).wait_recv()
        remote(meta.at[0], rm.at[s], m_send.at[0], m_recv.at[s], device).wait_recv()

    got = jnp.max(rm[...], axis=1)
    take = lax.broadcasted_iota(jnp.int32, (128, packed), 0)
    at = lax.broadcasted_iota(jnp.int32, (128, packed), 1) % pad
    mine = (lax.broadcasted_iota(jnp.int32, (devices, packed), 0)
            == lax.broadcasted_iota(jnp.int32, (devices, packed), 1) // pad)

    def lanes(offset):
        full = jnp.dot(got, (take == at + offset).astype(jnp.float32), precision=HIGHEST,
                       preferred_element_type=jnp.float32)
        return jnp.sum(jnp.where(mine, full, 0.0), axis=0, keepdims=True)

    scale_lane = lanes(0)
    slot_lane = jnp.round(lanes(64)).astype(jnp.int32)
    put = jnp.where(lax.broadcasted_iota(jnp.int32, (own, packed), 0) == slot_lane, scale_lane, 0.0).astype(jnp.bfloat16)
    high, low = split(ra[...].reshape(packed, rank))
    placed = (jnp.dot(put, high, preferred_element_type=jnp.float32)
              + jnp.dot(put, low, preferred_element_type=jnp.float32))
    out_ref[...] = jnp.dot(placed, ginv_ref[...], precision=HIGHEST, preferred_element_type=jnp.float32)

    @pl.loop(1, devices)
    def _(d):
        for copy in out_copies(d):
            copy.wait_send()


def per_device(n_row, n_col, tiles, tile_coord, tile_count, factors, owner, gram_inverse):
    own, rank = factors.shape
    tile_dim = tiles.shape[-1]
    slots = tiles.shape[2]
    devices = n_row * n_col
    row_tiles = own * n_col // tile_dim
    col_tiles = own * n_row // tile_dim
    tpd = own // tile_dim
    r = lax.axis_index("row")
    c = lax.axis_index("col")
    dma = pltpu.SemaphoreType.DMA

    row_panel, col_panel = pl.pallas_call(
        functools.partial(gather_kernel, n_row, n_col),
        out_shape=(
            jax.ShapeDtypeStruct((n_col, own, rank), factors.dtype),
            jax.ShapeDtypeStruct((n_row, own, rank), factors.dtype),
        ),
        in_specs=[ANY],
        out_specs=(ANY, ANY),
        scratch_shapes=[
            dma((n_col // 2,)), dma((n_col // 2,)), dma, dma((n_row,)),
            dma((n_col,)), dma((n_row,)), dma, dma((n_row,)),
        ],
        compiler_params=pltpu.CompilerParams(collective_id=0, has_side_effects=True),
        name="gather",
    )(factors)

    per_step = 8
    steps = slots // per_step
    count = tile_count[0, 0]
    numbers = jnp.stack([count, r * row_tiles, c * col_tiles]).astype(jnp.int32)
    whole = lambda *shape: pl.BlockSpec(shape, lambda g, a, b: (0,) * len(shape))
    qrow, qcol, srow, scol = pl.pallas_call(
        functools.partial(tile_kernel, per_step),
        out_shape=(
            jax.ShapeDtypeStruct((row_tiles, tile_dim, rank), jnp.int16),
            jax.ShapeDtypeStruct((col_tiles, tile_dim, rank), jnp.int16),
            jax.ShapeDtypeStruct((row_tiles, 1, tile_dim), jnp.float32),
            jax.ShapeDtypeStruct((col_tiles, 1, tile_dim), jnp.float32),
        ),
        grid_spec=pltpu.PrefetchScalarGridSpec(
            num_scalar_prefetch=2,
            grid=(steps,),
            in_specs=[
                pl.BlockSpec(
                    (per_step, tile_dim, tile_dim),
                    lambda g, a, b: (jnp.minimum(g, jnp.maximum(b[0] - 1, 0) // per_step), 0, 0),
                ),
                whole(row_tiles, tile_dim, rank),
                whole(col_tiles, tile_dim, rank),
            ],
            out_specs=(
                whole(row_tiles, tile_dim, rank),
                whole(col_tiles, tile_dim, rank),
                whole(row_tiles, 1, tile_dim),
                whole(col_tiles, 1, tile_dim),
            ),
            scratch_shapes=[
                pltpu.VMEM((row_tiles, tile_dim, rank), jnp.float32),
                pltpu.VMEM((col_tiles, tile_dim, rank), jnp.float32),
            ],
        ),
        compiler_params=pltpu.CompilerParams(vmem_limit_bytes=40 * MIB),
        name="tile_pass",
    )(
        tile_coord.reshape(-1), numbers, tiles.reshape(slots, tile_dim, tile_dim),
        row_panel.reshape(row_tiles, tile_dim, rank), col_panel.reshape(col_tiles, tile_dim, rank),
    )

    share = own // devices
    pad = -(-share // 16) * 16
    packed = devices * pad
    return pl.pallas_call(
        functools.partial(solve_kernel, n_row, n_col, pad, tile_dim),
        out_shape=jax.ShapeDtypeStruct((own, rank), jnp.float32),
        in_specs=[ANY, ANY, ANY, ANY, VMEM, VMEM, VMEM],
        out_specs=VMEM,
        scratch_shapes=[
            pltpu.VMEM((n_col, own, rank), jnp.int16),
            pltpu.VMEM((n_col * tpd, 1, tile_dim), jnp.float32),
            pltpu.VMEM((n_row, own, rank), jnp.int16),
            pltpu.VMEM((n_row * tpd, 1, tile_dim), jnp.float32),
            pltpu.VMEM((packed, own), jnp.float32),
            pltpu.VMEM((packed, rank), jnp.float32),
            pltpu.VMEM((devices, pad, rank), jnp.int16),
            pltpu.VMEM((devices, 8, 128), jnp.float32),
            pltpu.VMEM((devices, pad, rank), jnp.int16),
            pltpu.VMEM((devices, 8, 128), jnp.float32),
            dma((n_col,)), dma((n_col,)), dma((n_row,)), dma((n_row,)),
            dma((n_col,)), dma((n_col,)), dma((n_row,)), dma((n_row,)),
            dma((devices,)), dma((devices,)), dma((devices,)), dma((devices,)), dma((2,)),
        ],
        compiler_params=pltpu.CompilerParams(
            collective_id=1, has_side_effects=True, vmem_limit_bytes=40 * MIB),
        name="solve",
    )(
        qrow.reshape(n_col, own, rank), qcol.reshape(n_row, own, rank), srow, scol,
        owner.reshape(1, own), owner.reshape(own, 1), gram_inverse,
    )


def solution(mesh):
    in_specs = (
        P("row", "col", None, None, None),
        P("row", "col", None, None),
        P("row", "col"),
        P(("row", "col"), None),
        P(("row", "col")),
        P(),
    )
    out_specs = P(("row", "col"), None)
    return jax.shard_map(
        functools.partial(per_device, mesh.shape["row"], mesh.shape["col"]),
        mesh=mesh, in_specs=in_specs, out_specs=out_specs, check_vma=False,
    )
```

time: 386 us -> 178 us (0.46); the launches traced: 385 us -> 181 us
  Pallas kernels: 0 us -> 174 us
  waiting for transfers between devices: 170 us -> 0 us
  blocking collectives: 83.6 us -> 0 us
  local copies, waits for them, and re-layouts: 54.5 us -> 5.62 us
  matrix products: 35.6 us -> 0 us
  other arithmetic: 16.2 us -> 0.08 us
  between operations: 13.9 us -> 0.71 us
  starting transfers between devices: 10.2 us -> 0 us
    pallas_call x0 -> x3, Pallas kernels: none -> 174 us  [the longest x1 99.9 us: per_device(): pl.pallas_call(functools.partial(solve_kernel, n_row, n_col, pad, tile_di...]
    all_gather x1 -> x0, blocking collectives: 77 us -> none  [per_device(): lax.all_gather(owner, 'col', axis=0, tiled=True)]
    reduce_scatter x2 -> x0, waiting for transfers between devices: 61 us -> none  [the longest x1 54.1 us: per_device(): lax.psum_scatter(row_parts, 'col', scatter_dimension=0, tiled=True)]
    psum x1 -> x0, waiting for transfers between devices: 51.3 us -> none  [spread(): return lax.psum(jnp.where(mine, value, jnp.zeros_like(value)), axis)]
    dot_general x13 -> x0, matrix products: 35.6 us -> none  [the longest x3 12.5 us: block_step(): jnp.dot(row_select, row_terms.reshape(tiles_per_block, -1), precision=lax...]
    all_gather x1 -> x0, waiting for transfers between devices: 32.5 us -> none  [per_device(): lax.all_gather(factors, 'col', axis=0, tiled=True)]
    all_to_all x2 -> x0, waiting for transfers between devices: 24.9 us -> none  [the longest x1 24.9 us: per_device(): lax.all_to_all(moved, ('row', 'col'), split_axis=0, concat_axis=0, tiled=...]
    while x30 -> x0, local copies, waits for them, and re-layouts: 24.4 us -> none
  transfers between devices with their start and end apart: 6 -> 0, of which waited for: 5 -> 0; matrix products, arithmetic and copies ran while one was open for 5% -> 0% of each run, Pallas kernels for 0% -> 0%
where the time goes in v1:
time: 178 us; the launch traced here: 181 us
  Pallas kernels  174 us (98%)
  local copies, waits for them, and re-layouts  5.62 us (3%)
    pallas_call x1, Pallas kernels, per_device(): pl.pallas_call(functools.partial(solve_kernel, n_row, n_col, pad, tile_di...  99.9 us
    pallas_call x1, Pallas kernels, per_device(): pl.pallas_call(functools.partial(gather_kernel, n_row, n_col), out_shape=...  55.9 us
    pallas_call x1, Pallas kernels, per_device(): pl.pallas_call(functools.partial(tile_kernel, per_step), out_shape=(jax.S...  18.5 us
    unnamed x10, local copies, waits for them, and re-layouts  5.34 us

profile of v1, /device:TPU:0, one launch (start us, length us, event | category | flops | bytes accessed | tf_op | source)
XLA Modules:
  0.0 180.7 jit_solution(9246631363211965117)
XLA Ops:
  0.7 0.1 pad_add_fusion.meta_ref
  0.7 55.9 %gather.1 = (bf16[8,512,256]{2,1,0:T(8,128)(2,1)}, bf16[4,512,256]{2,1,0:T(8,128)(2,1)}) custom-call(bf16[512,256]{1,0:T(8,128)(2,1)} %f_ref.1), custom_call_target="tpu_custom_call" | custom-call | tf_op jit(solution)/shard_map/gather/pallas_call | solution.py:398
  56.6 0.8 copy.7
  57.4 0.1 reshape.24.coord_ref
  57.5 0.0 copy-start
  57.6 1.6 copy-done
  59.1 0.0 copy-start.1
  59.1 1.2 copy-done.1
  60.4 0.0 copy-start.3
  60.4 18.5 %tile_pass.1 = (s16[16,256,256]{2,1,0:T(8,128)(2,1)S(1)}, s16[8,256,256]{2,1,0:T(8,128)(2,1)S(1)}, f32[16,1,256]{2,1,0:T(1,128)S(1)}, f32[8,1,256]{2,1,0:T(1,128)S(1)}) custom-call(s32[192]{0:T(256)S(1)} %reshape.24.coord_ref, s32[3]{0:T(128)S(1)} %pad_add_fusion.meta_ref, bf16[96,256,256]{2,1,0:T(8,128)(2,1)} %bitcast.19, ...), custom_call_target="tpu_custom_call" | custom-call | tf_op jit(solution)/shard_map/tile_pass/pallas_call | solution.py:419
  78.9 0.0 copy-done.3
  78.9 0.1 copy.8.owner_sub
  79.0 0.0 copy-start.2
  79.1 0.9 copy-done.2
  80.0 99.9 %solve.1 = f32[512,256]{1,0:T(8,128)S(1)} custom-call(s16[8,512,256]{2,1,0:T(8,128)(2,1)S(1)} %bitcast.14, s16[4,512,256]{2,1,0:T(8,128)(2,1)S(1)} %bitcast.16, f32[16,1,256]{2,1,0:T(1,128)S(1)} %get-tuple-element.15.srow_ref, f32[8,1,256]{2,1,0:T(1,128)S(1)} %get-tuple-element.16.scol_ref, s32[1,512]{1,0:T(1,128)S(1)} %bitcast.18, ...), custom_call_target="tpu_custom_call" | custom-call | tf_op jit(solution)/shard_map/solve/pallas_call | solution.py:459
  179.9 0.8 copy.11
Async XLA Ops:
  57.5 1.6 copy-start
  59.1 1.2 copy-start.1
  60.4 18.5 %copy-start.3 = (s32[512]{0:T(512)S(1)}, s32[512]{0:T(512)}, u32[]{:S(2)}) copy-start(s32[512]{0:T(512)} %param.10) | copy-start | bytes 6148
  79.0 1.0 copy-start.2

commit v2 on v1

--- a/solution.py
+++ b/solution.py
@@ -21,8 +21,8 @@
     )
 
 
-def gather_kernel(n_row, n_col, f_ref, row_ref, col_ref, row_send, fwd_send, pair_send, col_send,
-                  row_recv, col_recv, local_sem, diag_sem):
+def gather_kernel(n_row, n_col, f_ref, row_ref, row_send, fwd_send, pair_send, col_send,
+                  row_recv, col_recv, local_sem):
     r = lax.axis_index("row")
     c = lax.axis_index("col")
     ratio = n_col // n_row
@@ -54,7 +54,7 @@
         return lax.rem(k + j, chips) >= r * ratio // 2
 
     def col_copy(d):
-        return remote(f_ref, col_ref.at[c % n_row], col_send.at[d], col_recv.at[c % n_row],
+        return remote(f_ref, row_ref.at[n_col + c % n_row], col_send.at[d], col_recv.at[c % n_row],
                       (r - d, r * ratio + c // n_row))
 
     for j in range(1, chips):
@@ -93,17 +93,6 @@
         for j in range(1, chips):
             forward(j).wait_send()
 
-    @pl.when(r == up)
-    def _():
-        copies = [
-            pltpu.make_async_copy(row_ref.at[(c % ratio) * n_row + i], col_ref.at[i], diag_sem.at[i])
-            for i in range(n_row)
-        ]
-        for copy in copies:
-            copy.start()
-        for copy in copies:
-            copy.wait()
-
     for j in range(1, chips):
         @pl.when(row_goes(j))
         def _(j=j):
@@ -116,7 +105,7 @@
     @pl.when(r < up)
     def _():
         for i in range(n_row):
-            remote(f_ref, col_ref.at[i], col_send.at[0], col_recv.at[i], (r, partner)).wait_recv()
+            remote(f_ref, row_ref.at[n_col + i], col_send.at[0], col_recv.at[i], (r, partner)).wait_recv()
 
 
 def encode(x):
@@ -136,32 +125,33 @@
     )
 
 
-def tile_kernel(per_step, coord_ref, meta_ref, tiles_ref, row_ref, col_ref,
+def tile_kernel(per_step, coord_ref, meta_ref, tiles_ref, panel_ref,
                 qrow_ref, qcol_ref, srow_ref, scol_ref, row_sum, col_sum):
     step = pl.program_id(0)
     count = meta_ref[0]
     tile_dim = tiles_ref.shape[-1]
+    row_tiles = qrow_ref.shape[0]
+    col_tiles = qcol_ref.shape[0]
 
     @pl.when(step == 0)
     def _():
         row_sum[...] = jnp.zeros_like(row_sum)
         col_sum[...] = jnp.zeros_like(col_sum)
 
-    for s in range(per_step):
-        slot = step * per_step + s
-
-        @pl.when(slot < count)
-        def _(s=s, slot=slot):
-            i = coord_ref[2 * slot]
-            j = coord_ref[2 * slot + 1]
+    @pl.when(step * per_step < count)
+    def _():
+        for s in range(per_step):
+            slot = step * per_step + s
+            live = slot < count
+            i = jnp.where(live, coord_ref[2 * slot], 0)
+            j = jnp.where(live, coord_ref[2 * slot + 1], 0)
+            upper = live & (meta_ref[1] + i < meta_ref[2] + j)
             tile = tiles_ref[s]
-            row_sum[i] += jnp.dot(tile, col_ref[j], preferred_element_type=jnp.float32)
-
-            @pl.when(meta_ref[1] + i < meta_ref[2] + j)
-            def _():
-                col_sum[j] += lax.dot_general(
-                    tile, row_ref[i], (((0,), (0,)), ((), ())), preferred_element_type=jnp.float32
-                )
+            row_term = jnp.dot(tile, panel_ref[meta_ref[3] + j], preferred_element_type=jnp.float32)
+            col_term = lax.dot_general(
+                tile, panel_ref[i], (((0,), (0,)), ((), ())), preferred_element_type=jnp.float32)
+            row_sum[jnp.where(live, i, row_tiles)] += row_term
+            col_sum[jnp.where(upper, j, col_tiles)] += col_term
 
     @pl.when(step == pl.num_programs(0) - 1)
     def _():
@@ -169,7 +159,7 @@
                == lax.broadcasted_iota(jnp.int32, (tile_dim, tile_dim), 1))
 
         def code(total, coded_ref, scale_ref):
-            @pl.loop(0, total.shape[0])
+            @pl.loop(0, coded_ref.shape[0], unroll=4)
             def _(t):
                 coded, scale = encode(total[t])
                 coded_ref[t] = coded
@@ -180,9 +170,9 @@
 
 
 def solve_kernel(n_row, n_col, pad, tile_dim, qrow_ref, qcol_ref, srow_ref, scol_ref, owner_lane, owner_sub, ginv_ref,
-                 out_ref, rq, rs, cq, cs, pick, total, qa, meta, ra, rm,
+                 out_ref, rq, rs, cq, cs, hq, hs, pick, total, qa, meta, ra, rm,
                  row_send, rsc_send, col_send, csc_send, row_recv, rsc_recv, col_recv, csc_recv,
-                 a_send, m_send, a_recv, m_recv, local_sem):
+                 hq_send, hs_send, hq_recv, hs_recv, a_send, m_send, a_recv, m_recv, local_sem):
     r = lax.axis_index("row")
     c = lax.axis_index("col")
     me = r * n_col + c
@@ -210,6 +200,29 @@
                    rsc_send.at[j], rsc_recv.at[c], (r, to)),
         )
 
+    def relay_copies(i):
+        to = (r, (c % ratio) * n_row + i)
+        return (
+            remote(qcol_ref.at[i], hq.at[up], col_send.at[i], hq_recv.at[up], to),
+            remote(scol_ref.at[pl.ds(i * tpd, tpd)], hs.at[pl.ds(up * tpd, tpd)],
+                   csc_send.at[i], hs_recv.at[up], to),
+        )
+
+    def relay_arrival(u):
+        device = (r, ratio * u + c // n_row)
+        remote(qcol_ref.at[0], hq.at[u], col_send.at[0], hq_recv.at[u], device).wait_recv()
+        remote(scol_ref.at[pl.ds(0, tpd)], hs.at[pl.ds(u * tpd, tpd)], csc_send.at[0], hs_recv.at[u],
+               device).wait_recv()
+
+    def hop_copies(u):
+        return (
+            remote(hq.at[u], cq.at[r], hq_send.at[u], col_recv.at[r], (u, c)),
+            remote(hs.at[pl.ds(u * tpd, tpd)], cs.at[pl.ds(r * tpd, tpd)], hs_send.at[u], csc_recv.at[r], (u, c)),
+        )
+
+    def hops(u):
+        return (u > r) & (ratio * u + c // n_row != c)
+
     def col_copies(i):
         to = (up, (c % ratio) * n_row + i)
         return (
@@ -224,8 +237,17 @@
             pltpu.make_async_copy(scol_ref.at[pl.ds(i * tpd, tpd)], cs.at[pl.ds(r * tpd, tpd)], csc_recv.at[r]),
         )
 
+    def stays(i):
+        return (c % ratio) * n_row + i == c
+
     def col_mine(i):
-        return (r == up) & ((c % ratio) * n_row + i == c)
+        return (r == up) & stays(i)
+
+    def col_relayed(i):
+        return (r < up) & jnp.logical_not(stays(i))
+
+    def col_direct(i):
+        return (r <= up) & jnp.logical_not(col_mine(i)) & jnp.logical_not(col_relayed(i))
 
     row_here = (
         pltpu.make_async_copy(qrow_ref.at[c], rq.at[c], row_recv.at[c]),
@@ -235,7 +257,12 @@
     @pl.when(used)
     def _():
         for i in range(n_row):
-            @pl.when(jnp.logical_not(col_mine(i)))
+            @pl.when(col_relayed(i))
+            def _(i=i):
+                for copy in relay_copies(i):
+                    copy.start()
+
+            @pl.when(col_direct(i))
             def _(i=i):
                 for copy in col_copies(i):
                     copy.start()
@@ -261,6 +288,13 @@
     slot_sub = jnp.sum(jnp.where(chosen, slot, 0.0), axis=1, keepdims=True)
     total[...] = jnp.zeros_like(total)
 
+    for u in range(n_row - 1, 0, -1):
+        @pl.when(hops(u))
+        def _(u=u):
+            relay_arrival(u)
+            for copy in hop_copies(u):
+                copy.start()
+
     def add(coded_ref, scales_ref, s):
         for t in range(tpd):
             words = pl.ds(t * tile_dim, tile_dim)
@@ -285,6 +319,14 @@
             copy.wait()
         add(rq, rs, c)
 
+    for j in range(1, n_col):
+        s = lax.rem(c - j + n_col, n_col)
+
+        @pl.when(s >= r * ratio)
+        def _(s=s):
+            row_arrival(s)
+            add(rq, rs, s)
+
     for d in range(n_row):
         @pl.when(r - d >= 0)
         def _(d=d):
@@ -302,14 +344,6 @@
             else:
                 col_arrival(r - d)
             add(cq, cs, r - d)
-
-    for j in range(1, n_col):
-        s = lax.rem(c - j + n_col, n_col)
-
-        @pl.when(s >= r * ratio)
-        def _(s=s):
-            row_arrival(s)
-            add(rq, rs, s)
 
     coded, scale = encode(total[...])
     qa[...] = coded.reshape(devices, pad, rank)
@@ -343,12 +377,23 @@
     @pl.when(used)
     def _():
         for i in range(n_row):
-            @pl.when(jnp.logical_not(col_mine(i)))
+            @pl.when(col_relayed(i))
+            def _(i=i):
+                for copy in relay_copies(i):
+                    copy.wait_send()
+
+            @pl.when(col_direct(i))
             def _(i=i):
                 for copy in col_copies(i):
                     copy.wait_send()
         for j in range(1, n_col):
             for copy in row_copies(j):
+                copy.wait_send()
+
+    for u in range(n_row - 1, 0, -1):
+        @pl.when(hops(u))
+        def _(u=u):
+            for copy in hop_copies(u):
                 copy.wait_send()
 
     @pl.loop(1, devices)
@@ -395,17 +440,14 @@
     c = lax.axis_index("col")
     dma = pltpu.SemaphoreType.DMA
 
-    row_panel, col_panel = pl.pallas_call(
+    panel = pl.pallas_call(
         functools.partial(gather_kernel, n_row, n_col),
-        out_shape=(
-            jax.ShapeDtypeStruct((n_col, own, rank), factors.dtype),
-            jax.ShapeDtypeStruct((n_row, own, rank), factors.dtype),
-        ),
+        out_shape=jax.ShapeDtypeStruct((n_col + n_row, own, rank), factors.dtype),
         in_specs=[ANY],
-        out_specs=(ANY, ANY),
+        out_specs=ANY,
         scratch_shapes=[
             dma((n_col // 2,)), dma((n_col // 2,)), dma, dma((n_row,)),
-            dma((n_col,)), dma((n_row,)), dma, dma((n_row,)),
+            dma((n_col,)), dma((n_row,)), dma,
         ],
         compiler_params=pltpu.CompilerParams(collective_id=0, has_side_effects=True),
         name="gather",
@@ -414,7 +456,9 @@
     per_step = 8
     steps = slots // per_step
     count = tile_count[0, 0]
-    numbers = jnp.stack([count, r * row_tiles, c * col_tiles]).astype(jnp.int32)
+    ratio = n_col // n_row
+    first = jnp.where(r == c // ratio, (c % ratio) * col_tiles, row_tiles)
+    numbers = jnp.stack([count, r * row_tiles, c * col_tiles, first]).astype(jnp.int32)
     whole = lambda *shape: pl.BlockSpec(shape, lambda g, a, b: (0,) * len(shape))
     qrow, qcol, srow, scol = pl.pallas_call(
         functools.partial(tile_kernel, per_step),
@@ -432,8 +476,7 @@
                     (per_step, tile_dim, tile_dim),
                     lambda g, a, b: (jnp.minimum(g, jnp.maximum(b[0] - 1, 0) // per_step), 0, 0),
                 ),
-                whole(row_tiles, tile_dim, rank),
-                whole(col_tiles, tile_dim, rank),
+                whole(row_tiles + col_tiles, tile_dim, rank),
             ],
             out_specs=(
                 whole(row_tiles, tile_dim, rank),
@@ -442,15 +485,15 @@
                 whole(col_tiles, 1, tile_dim),
             ),
             scratch_shapes=[
-                pltpu.VMEM((row_tiles, tile_dim, rank), jnp.float32),
-                pltpu.VMEM((col_tiles, tile_dim, rank), jnp.float32),
+                pltpu.VMEM((row_tiles + 1, tile_dim, rank), jnp.float32),
+                pltpu.VMEM((col_tiles + 1, tile_dim, rank), jnp.float32),
             ],
         ),
-        compiler_params=pltpu.CompilerParams(vmem_limit_bytes=40 * MIB),
+        compiler_params=pltpu.CompilerParams(vmem_limit_bytes=56 * MIB),
         name="tile_pass",
     )(
         tile_coord.reshape(-1), numbers, tiles.reshape(slots, tile_dim, tile_dim),
-        row_panel.reshape(row_tiles, tile_dim, rank), col_panel.reshape(col_tiles, tile_dim, rank),
+        panel.reshape(row_tiles + col_tiles, tile_dim, rank),
     )
 
     share = own // devices
@@ -466,6 +509,8 @@
             pltpu.VMEM((n_col * tpd, 1, tile_dim), jnp.float32),
             pltpu.VMEM((n_row, own, rank), jnp.int16),
             pltpu.VMEM((n_row * tpd, 1, tile_dim), jnp.float32),
+            pltpu.VMEM((n_row, own, rank), jnp.int16),
+            pltpu.VMEM((n_row * tpd, 1, tile_dim), jnp.float32),
             pltpu.VMEM((packed, own), jnp.float32),
             pltpu.VMEM((packed, rank), jnp.float32),
             pltpu.VMEM((devices, pad, rank), jnp.int16),
@@ -474,6 +519,7 @@
             pltpu.VMEM((devices, 8, 128), jnp.float32),
             dma((n_col,)), dma((n_col,)), dma((n_row,)), dma((n_row,)),
             dma((n_col,)), dma((n_col,)), dma((n_row,)), dma((n_row,)),
+            dma((n_row,)), dma((n_row,)), dma((n_row,)), dma((n_row,)),
             dma((devices,)), dma((devices,)), dma((devices,)), dma((devices,)), dma((2,)),
         ],
         compiler_params=pltpu.CompilerParams(

time: 178 us -> 112 us (0.63); the launches traced: 181 us -> 111 us
  Pallas kernels: 174 us -> 104 us
    pallas_call x1, Pallas kernels: 99.9 us -> 63.3 us  [per_device(): pl.pallas_call(functools.partial(solve_kernel, n_row, n_col, pad, tile_di...]
    pallas_call x1, Pallas kernels: 55.9 us -> 28.7 us  [per_device(): pl.pallas_call(functools.partial(gather_kernel, n_row, n_col), out_shape=...]
    pallas_call x1, Pallas kernels: 18.5 us -> 12.1 us  [per_device(): pl.pallas_call(functools.partial(tile_kernel, per_step), out_shape=(jax.S...]
    unnamed x10 -> x16, local copies, waits for them, and re-layouts: 5.34 us -> 5.13 us
where the time goes in v2:
time: 112 us; the launch traced here: 111 us
  Pallas kernels  104 us (93%)
  local copies, waits for them, and re-layouts  6.01 us (5%)
    pallas_call x1, Pallas kernels, per_device(): pl.pallas_call(functools.partial(solve_kernel, n_row, n_col, pad, tile_di...  63.3 us
    pallas_call x1, Pallas kernels, per_device(): pl.pallas_call(functools.partial(gather_kernel, n_row, n_col), out_shape=...  28.7 us
    pallas_call x1, Pallas kernels, per_device(): pl.pallas_call(functools.partial(tile_kernel, per_step), out_shape=(jax.S...  12.1 us
    unnamed x16, local copies, waits for them, and re-layouts  5.13 us

profile of v2, /device:TPU:0, one launch (start us, length us, event | category | flops | bytes accessed | tf_op | source)
XLA Modules:
  0.0 111.4 jit_solution(13448937942294279423)
XLA Ops:
  0.0 0.0 copy-start.6
  0.7 0.6 pad_add_fusion.meta_ref
  1.3 28.7 %gather.1 = bf16[12,512,256]{2,1,0:T(8,128)(2,1)} custom-call(bf16[512,256]{1,0:T(8,128)(2,1)} %f_ref.1), custom_call_target="tpu_custom_call" | custom-call | tf_op jit(solution)/shard_map/gather/pallas_call | solution.py:443
  30.0 0.0 copy-done.6
  30.0 0.1 copy.7
  30.2 0.7 reshape.21.coord_ref
  30.9 0.0 copy-start.5
  30.9 0.0 copy-start.2
  30.9 12.1 %tile_pass.1 = (s16[16,256,256]{2,1,0:T(8,128)(2,1)}, s16[8,256,256]{2,1,0:T(8,128)(2,1)}, f32[16,1,256]{2,1,0:T(1,128)}, f32[8,1,256]{2,1,0:T(1,128)}) custom-call(s32[192]{0:T(256)} %reshape.21.coord_ref, s32[4]{0:T(128)} %pad_add_fusion.meta_ref, bf16[96,256,256]{2,1,0:T(8,128)(2,1)} %bitcast.17, bf16[24,256,256]{2,1,0:T(8,128)(2,1)} %bitcast.18), custom_call_target="tpu_custom_call" | custom-call | tf_op jit(solution)/shard_map/tile_pass/pallas_call | solution.py:463
  43.0 0.0 copy-done.5
  43.0 0.1 copy.8.owner_sub
  43.1 0.0 copy-done.2
  43.1 0.0 copy-start
  43.1 1.6 %copy-done = s16[16,256,256]{2,1,0:T(8,128)(2,1)S(1)} copy-done((s16[16,256,256]{2,1,0:T(8,128)(2,1)S(1)}, s16[16,256,256]{2,1,0:T(8,128)(2,1)}, u32[]{:S(2)}) %copy-start) | copy-done | bytes 2097176
  44.7 0.0 copy-start.1
  44.7 1.2 %copy-done.1 = s16[8,256,256]{2,1,0:T(8,128)(2,1)S(1)} copy-done((s16[8,256,256]{2,1,0:T(8,128)(2,1)S(1)}, s16[8,256,256]{2,1,0:T(8,128)(2,1)}, u32[]{:S(2)}) %copy-start.1) | copy-done | bytes 1048600
  45.9 0.0 copy-start.3
  45.9 0.7 copy-done.3
  46.7 0.0 copy-start.4
  46.7 0.7 copy-done.4
  47.4 63.3 %solve.1 = f32[512,256]{1,0:T(8,128)S(1)} custom-call(s16[8,512,256]{2,1,0:T(8,128)(2,1)S(1)} %bitcast.13, s16[4,512,256]{2,1,0:T(8,128)(2,1)S(1)} %bitcast.14, f32[16,1,256]{2,1,0:T(1,128)S(1)} %copy-done.3, f32[8,1,256]{2,1,0:T(1,128)S(1)} %copy-done.4, s32[1,512]{1,0:T(1,128)S(1)} %bitcast.16, s32[512,1]{1,0:T(8,128)S(1)} %copy.8.owner_sub, ...), custom_call_target="tpu_custom_call" | custom-call | tf_op jit(solution)/shard_map/solve/pallas_call | solution.py:502
  110.6 0.8 copy.11
Async XLA Ops:
  0.0 30.0 %copy-start.6 = (s32[1,1,96,2]{2,3,1,0:T(2,128)S(1)}, s32[1,1,96,2]{2,3,1,0:T(2,128)}, u32[]{:S(2)}) copy-start(s32[1,1,96,2]{2,3,1,0:T(2,128)} %param.7) | copy-start | bytes 2308
  30.9 12.1 %copy-start.5 = (s32[512]{0:T(512)S(1)}, s32[512]{0:T(512)}, u32[]{:S(2)}) copy-start(s32[512]{0:T(512)} %param.10) | copy-start | bytes 6148
  30.9 12.2 %copy-start.2 = (f32[256,256]{1,0:T(8,128)S(1)}, f32[256,256]{1,0:T(8,128)}, u32[]{:S(2)}) copy-start(f32[256,256]{1,0:T(8,128)} %ginv_ref.1) | copy-start | bytes 786436
  43.1 1.6 %copy-start = (s16[16,256,256]{2,1,0:T(8,128)(2,1)S(1)}, s16[16,256,256]{2,1,0:T(8,128)(2,1)}, u32[]{:S(2)}) copy-start(s16[16,256,256]{2,1,0:T(8,128)(2,1)} %get-tuple-element.9) | copy-start | bytes 6291460
  44.7 1.2 %copy-start.1 = (s16[8,256,256]{2,1,0:T(8,128)(2,1)S(1)}, s16[8,256,256]{2,1,0:T(8,128)(2,1)}, u32[]{:S(2)}) copy-start(s16[8,256,256]{2,1,0:T(8,128)(2,1)} %get-tuple-element.10) | copy-start | bytes 3145732
  45.9 0.7 copy-start.3
  46.7 0.7 copy-start.4

commit v3 on v2

--- a/solution.py
+++ b/solution.py
@@ -12,6 +12,7 @@
 VMEM = pl.BlockSpec(memory_space=pltpu.VMEM)
 HIGHEST = lax.Precision.HIGHEST
 MIB = 1 << 20
+PARTS = 4
 
 
 def remote(src, dst, send_sem, recv_sem, device):
@@ -170,8 +171,8 @@
 
 
 def solve_kernel(n_row, n_col, pad, tile_dim, qrow_ref, qcol_ref, srow_ref, scol_ref, owner_lane, owner_sub, ginv_ref,
-                 out_ref, rq, rs, cq, cs, hq, hs, pick, total, qa, meta, ra, rm,
-                 row_send, rsc_send, col_send, csc_send, row_recv, rsc_recv, col_recv, csc_recv,
+                 out_ref, rq, rs, oq, pq, ps, eq, es, cq, cs, hq, hs, pick, total, qa, meta, ra, rm,
+                 pq_send, ps_send, pq_recv, ps_recv, oq_sem, row_send, rsc_send, col_send, csc_send, row_recv, rsc_recv, col_recv, csc_recv,
                  hq_send, hs_send, hq_recv, hs_recv, a_send, m_send, a_recv, m_recv, local_sem):
     r = lax.axis_index("row")
     c = lax.axis_index("col")
@@ -192,48 +193,70 @@
         pl.semaphore_signal(barrier, inc=1, device_id=(to // n_col, to % n_col), device_id_type=MESH)
     pl.semaphore_wait(barrier, devices - 1)
 
-    def row_copies(j):
-        to = lax.rem(c + j, n_col)
+    chips = n_col // 2
+    k, e = c // 2, c % 2
+    partner = c + 1 - 2 * e
+
+    def tiles_of(m):
+        return pl.ds(m * tpd, tpd)
+
+    def pair_copies(m):
+        to = 2 * m + 1 - e
         return (
-            remote(qrow_ref.at[to], rq.at[c], row_send.at[j], row_recv.at[c], (r, to)),
-            remote(srow_ref.at[pl.ds(to * tpd, tpd)], rs.at[pl.ds(c * tpd, tpd)],
-                   rsc_send.at[j], rsc_recv.at[c], (r, to)),
+            remote(qrow_ref.at[to], pq.at[m], pq_send.at[m], pq_recv.at[m], (r, partner)),
+            remote(srow_ref.at[tiles_of(to)], ps.at[tiles_of(m)], ps_send.at[m], ps_recv.at[m], (r, partner)),
         )
 
-    def relay_copies(i):
+    def own_copy(m):
+        return pltpu.make_async_copy(qrow_ref.at[2 * m + e], oq.at[m], oq_sem.at[m])
+
+    def row_copies(m):
+        to = (r, 2 * m + e)
+        return (
+            remote(eq.at[m], rq.at[k], row_send.at[m], row_recv.at[k], to),
+            remote(es.at[tiles_of(m)], rs.at[tiles_of(k)], rsc_send.at[m], rsc_recv.at[k], to),
+        )
+
+    def rows_of(p):
+        return pl.ds(p * (own // PARTS), own // PARTS)
+
+    def relay_copies(i, p):
         to = (r, (c % ratio) * n_row + i)
-        return (
-            remote(qcol_ref.at[i], hq.at[up], col_send.at[i], hq_recv.at[up], to),
-            remote(scol_ref.at[pl.ds(i * tpd, tpd)], hs.at[pl.ds(up * tpd, tpd)],
-                   csc_send.at[i], hs_recv.at[up], to),
-        )
-
-    def relay_arrival(u):
+        values = remote(qcol_ref.at[i, rows_of(p)], hq.at[up, rows_of(p)],
+                        col_send.at[i, p], hq_recv.at[up, p], to)
+        scales = remote(scol_ref.at[pl.ds(i * tpd, tpd)], hs.at[pl.ds(up * tpd, tpd)],
+                        csc_send.at[i], hs_recv.at[up], to)
+        return (scales, values) if p == 0 else (values,)
+
+    def hop_copies(u, p):
+        values = remote(hq.at[u, rows_of(p)], cq.at[r, rows_of(p)], hq_send.at[u, p], col_recv.at[r, p], (u, c))
+        scales = remote(hs.at[pl.ds(u * tpd, tpd)], cs.at[pl.ds(r * tpd, tpd)],
+                        hs_send.at[u], csc_recv.at[r], (u, c))
+        return (scales, values) if p == 0 else (values,)
+
+    def relay_arrival(u, p):
         device = (r, ratio * u + c // n_row)
-        remote(qcol_ref.at[0], hq.at[u], col_send.at[0], hq_recv.at[u], device).wait_recv()
-        remote(scol_ref.at[pl.ds(0, tpd)], hs.at[pl.ds(u * tpd, tpd)], csc_send.at[0], hs_recv.at[u],
+        remote(qcol_ref.at[0, rows_of(p)], hq.at[u, rows_of(p)], col_send.at[0, p], hq_recv.at[u, p],
                device).wait_recv()
-
-    def hop_copies(u):
-        return (
-            remote(hq.at[u], cq.at[r], hq_send.at[u], col_recv.at[r], (u, c)),
-            remote(hs.at[pl.ds(u * tpd, tpd)], cs.at[pl.ds(r * tpd, tpd)], hs_send.at[u], csc_recv.at[r], (u, c)),
-        )
+        if p == 0:
+            remote(scol_ref.at[pl.ds(0, tpd)], hs.at[pl.ds(u * tpd, tpd)], csc_send.at[0], hs_recv.at[u],
+                   device).wait_recv()
 
     def hops(u):
         return (u > r) & (ratio * u + c // n_row != c)
 
-    def col_copies(i):
+    def col_copies(i, p):
         to = (up, (c % ratio) * n_row + i)
-        return (
-            remote(qcol_ref.at[i], cq.at[r], col_send.at[i], col_recv.at[r], to),
-            remote(scol_ref.at[pl.ds(i * tpd, tpd)], cs.at[pl.ds(r * tpd, tpd)],
-                   csc_send.at[i], csc_recv.at[r], to),
-        )
+        values = remote(qcol_ref.at[i, rows_of(p)], cq.at[r, rows_of(p)], col_send.at[i, p], col_recv.at[r, p], to)
+        scales = remote(scol_ref.at[pl.ds(i * tpd, tpd)], cs.at[pl.ds(r * tpd, tpd)],
+                        csc_send.at[i], csc_recv.at[r], to)
+        return (scales, values) if p == 0 else (values,)
 
     def col_here(i):
-        return (
-            pltpu.make_async_copy(qcol_ref.at[i], cq.at[r], col_recv.at[r]),
+        return tuple(
+            pltpu.make_async_copy(qcol_ref.at[i, rows_of(p)], cq.at[r, rows_of(p)], col_recv.at[r, p])
+            for p in range(PARTS)
+        ) + (
             pltpu.make_async_copy(scol_ref.at[pl.ds(i * tpd, tpd)], cs.at[pl.ds(r * tpd, tpd)], csc_recv.at[r]),
         )
 
@@ -249,33 +272,29 @@
     def col_direct(i):
         return (r <= up) & jnp.logical_not(col_mine(i)) & jnp.logical_not(col_relayed(i))
 
-    row_here = (
-        pltpu.make_async_copy(qrow_ref.at[c], rq.at[c], row_recv.at[c]),
-        pltpu.make_async_copy(srow_ref.at[pl.ds(c * tpd, tpd)], rs.at[pl.ds(c * tpd, tpd)], rsc_recv.at[c]),
-    )
-
     @pl.when(used)
     def _():
+        for p in range(PARTS):
+            for i in range(n_row):
+                @pl.when(col_relayed(i))
+                def _(i=i, p=p):
+                    for copy in relay_copies(i, p):
+                        copy.start()
+
+                @pl.when(col_direct(i))
+                def _(i=i, p=p):
+                    for copy in col_copies(i, p):
+                        copy.start()
         for i in range(n_row):
-            @pl.when(col_relayed(i))
-            def _(i=i):
-                for copy in relay_copies(i):
-                    copy.start()
-
-            @pl.when(col_direct(i))
-            def _(i=i):
-                for copy in col_copies(i):
-                    copy.start()
-
             @pl.when(col_mine(i))
             def _(i=i):
                 for copy in col_here(i):
                     copy.start()
-        for j in range(1, n_col):
-            for copy in row_copies(j):
+        for j in range(1, chips + 1):
+            m = lax.rem(k + j, chips)
+            own_copy(m).start()
+            for copy in pair_copies(m):
                 copy.start()
-        for copy in row_here:
-            copy.start()
 
     ow = owner_lane[...]
     dest = ow // own
@@ -288,41 +307,75 @@
     slot_sub = jnp.sum(jnp.where(chosen, slot, 0.0), axis=1, keepdims=True)
     total[...] = jnp.zeros_like(total)
 
-    for u in range(n_row - 1, 0, -1):
-        @pl.when(hops(u))
-        def _(u=u):
-            relay_arrival(u)
-            for copy in hop_copies(u):
+    eye = (lax.broadcasted_iota(jnp.int32, (tile_dim, tile_dim), 0)
+           == lax.broadcasted_iota(jnp.int32, (tile_dim, tile_dim), 1))
+
+    def decode(coded, scale):
+        down = jnp.sum(jnp.where(eye, scale, 0.0), axis=1, keepdims=True)
+        return coded.astype(jnp.int32).astype(jnp.float32) * down
+
+    def pair_sum(j):
+        @pl.when(used)
+        def _():
+            m = lax.rem(k + j, chips)
+            own_copy(m).wait()
+            for copy in pair_copies(m):
+                copy.wait_recv()
+            for t in range(tpd):
+                words = pl.ds(t * tile_dim, tile_dim)
+                both = (decode(oq[m, words, :], srow_ref[(2 * m + e) * tpd + t])
+                        + decode(pq[m, words, :], ps[m * tpd + t]))
+                coded, scale = encode(both)
+                eq[m, words, :] = coded
+                es[m * tpd + t] = jnp.sum(jnp.where(eye, scale, 0.0), axis=0, keepdims=True)
+            for copy in row_copies(m):
                 copy.start()
 
-    def add(coded_ref, scales_ref, s):
+    def relay(p):
+        for u in range(n_row - 1, 0, -1):
+            @pl.when(hops(u))
+            def _(u=u):
+                relay_arrival(u, p)
+                for copy in hop_copies(u, p):
+                    copy.start()
+
+    for n in range(max(chips - 1, PARTS)):
+        if n < chips - 1:
+            pair_sum(n + 1)
+        if n < PARTS:
+            relay(n)
+
+    def add(coded_ref, scales_ref, s, at=None):
         for t in range(tpd):
             words = pl.ds(t * tile_dim, tile_dim)
-            scaled = (pick[:, words] * scales_ref[s * tpd + t]).astype(jnp.bfloat16)
+            scaled = (pick[:, words] * scales_ref[(s if at is None else at) * tpd + t]).astype(jnp.bfloat16)
             high, low = split(coded_ref[s, words, :])
             total[...] += (jnp.dot(scaled, high, preferred_element_type=jnp.float32)
                            + jnp.dot(scaled, low, preferred_element_type=jnp.float32))
 
     def row_arrival(s):
-        remote(qrow_ref.at[0], rq.at[s], row_send.at[0], row_recv.at[s], (r, s)).wait_recv()
-        remote(srow_ref.at[pl.ds(0, tpd)], rs.at[pl.ds(s * tpd, tpd)], rsc_send.at[0], rsc_recv.at[s],
-               (r, s)).wait_recv()
+        remote(eq.at[0], rq.at[s], row_send.at[0], row_recv.at[s], (r, 2 * s + e)).wait_recv()
+        remote(es.at[tiles_of(0)], rs.at[tiles_of(s)], rsc_send.at[0], rsc_recv.at[s], (r, 2 * s + e)).wait_recv()
 
     def col_arrival(s):
-        remote(qcol_ref.at[0], cq.at[s], col_send.at[0], col_recv.at[s], (s, c)).wait_recv()
+        for p in range(PARTS):
+            remote(qcol_ref.at[0, rows_of(p)], cq.at[s, rows_of(p)], col_send.at[0, p], col_recv.at[s, p],
+                   (s, c)).wait_recv()
         remote(scol_ref.at[pl.ds(0, tpd)], cs.at[pl.ds(s * tpd, tpd)], csc_send.at[0], csc_recv.at[s],
                (s, c)).wait_recv()
 
     @pl.when(used)
     def _():
-        for copy in row_here:
-            copy.wait()
-        add(rq, rs, c)
-
-    for j in range(1, n_col):
-        s = lax.rem(c - j + n_col, n_col)
-
-        @pl.when(s >= r * ratio)
+        own_copy(k).wait()
+        for copy in pair_copies(k):
+            copy.wait_recv()
+        add(oq, srow_ref, k, c)
+        add(pq, ps, k)
+
+    for j in range(1, chips):
+        s = lax.rem(k - j + chips, chips)
+
+        @pl.when(s >= r * ratio // 2)
         def _(s=s):
             row_arrival(s)
             add(rq, rs, s)
@@ -379,22 +432,28 @@
         for i in range(n_row):
             @pl.when(col_relayed(i))
             def _(i=i):
-                for copy in relay_copies(i):
-                    copy.wait_send()
+                for p in range(PARTS):
+                    for copy in relay_copies(i, p):
+                        copy.wait_send()
 
             @pl.when(col_direct(i))
             def _(i=i):
-                for copy in col_copies(i):
-                    copy.wait_send()
-        for j in range(1, n_col):
-            for copy in row_copies(j):
+                for p in range(PARTS):
+                    for copy in col_copies(i, p):
+                        copy.wait_send()
+        for j in range(1, chips):
+            for copy in row_copies(lax.rem(k + j, chips)):
+                copy.wait_send()
+        for m in range(chips):
+            for copy in pair_copies(m):
                 copy.wait_send()
 
     for u in range(n_row - 1, 0, -1):
         @pl.when(hops(u))
         def _(u=u):
-            for copy in hop_copies(u):
-                copy.wait_send()
+            for p in range(PARTS):
+                for copy in hop_copies(u, p):
+                    copy.wait_send()
 
     @pl.loop(1, devices)
     def _(d):
@@ -497,16 +556,22 @@
     )
 
     share = own // devices
+    chips = n_col // 2
     pad = -(-share // 16) * 16
     packed = devices * pad
     return pl.pallas_call(
         functools.partial(solve_kernel, n_row, n_col, pad, tile_dim),
         out_shape=jax.ShapeDtypeStruct((own, rank), jnp.float32),
-        in_specs=[ANY, ANY, ANY, ANY, VMEM, VMEM, VMEM],
+        in_specs=[ANY, ANY, VMEM, ANY, VMEM, VMEM, VMEM],
         out_specs=VMEM,
         scratch_shapes=[
-            pltpu.VMEM((n_col, own, rank), jnp.int16),
-            pltpu.VMEM((n_col * tpd, 1, tile_dim), jnp.float32),
+            pltpu.VMEM((chips, own, rank), jnp.int16),
+            pltpu.VMEM((chips * tpd, 1, tile_dim), jnp.float32),
+            pltpu.VMEM((chips, own, rank), jnp.int16),
+            pltpu.VMEM((chips, own, rank), jnp.int16),
+            pltpu.VMEM((chips * tpd, 1, tile_dim), jnp.float32),
+            pltpu.VMEM((chips, own, rank), jnp.int16),
+            pltpu.VMEM((chips * tpd, 1, tile_dim), jnp.float32),
             pltpu.VMEM((n_row, own, rank), jnp.int16),
             pltpu.VMEM((n_row * tpd, 1, tile_dim), jnp.float32),
             pltpu.VMEM((n_row, own, rank), jnp.int16),
@@ -517,13 +582,14 @@
             pltpu.VMEM((devices, 8, 128), jnp.float32),
             pltpu.VMEM((devices, pad, rank), jnp.int16),
             pltpu.VMEM((devices, 8, 128), jnp.float32),
-            dma((n_col,)), dma((n_col,)), dma((n_row,)), dma((n_row,)),
-            dma((n_col,)), dma((n_col,)), dma((n_row,)), dma((n_row,)),
-            dma((n_row,)), dma((n_row,)), dma((n_row,)), dma((n_row,)),
+            dma((chips,)), dma((chips,)), dma((chips,)), dma((chips,)), dma((chips,)),
+            dma((chips,)), dma((chips,)), dma((n_row, PARTS)), dma((n_row,)),
+            dma((chips,)), dma((chips,)), dma((n_row, PARTS)), dma((n_row,)),
+            dma((n_row, PARTS)), dma((n_row,)), dma((n_row, PARTS)), dma((n_row,)),
             dma((devices,)), dma((devices,)), dma((devices,)), dma((devices,)), dma((2,)),
         ],
         compiler_params=pltpu.CompilerParams(
-            collective_id=1, has_side_effects=True, vmem_limit_bytes=40 * MIB),
+            collective_id=1, has_side_effects=True, vmem_limit_bytes=60 * MIB),
         name="solve",
     )(
         qrow.reshape(n_col, own, rank), qcol.reshape(n_row, own, rank), srow, scol,

time: 112 us -> 105 us (0.938)
  Pallas kernels: 104 us -> 98.5 us
  local copies, waits for them, and re-layouts: 6.01 us -> 3.54 us
    pallas_call x1, Pallas kernels: 63.3 us -> 57.6 us  [per_device(): pl.pallas_call(functools.partial(solve_kernel, n_row, n_col, pad, tile_di...]
    unnamed x16 -> x6, local copies, waits for them, and re-layouts: 5.13 us -> 1.98 us
where the time goes in v3:
time: 105 us; the launch traced here: 103 us
  Pallas kernels  98.5 us (94%)
  local copies, waits for them, and re-layouts  3.54 us (3%)
    pallas_call x1, Pallas kernels, per_device(): pl.pallas_call(functools.partial(solve_kernel, n_row, n_col, pad, tile_di...  57.6 us
    pallas_call x1, Pallas kernels, per_device(): pl.pallas_call(functools.partial(gather_kernel, n_row, n_col), out_shape=...  28.7 us
    pallas_call x1, Pallas kernels, per_device(): pl.pallas_call(functools.partial(tile_kernel, per_step), out_shape=(jax.S...  12.1 us

profile of v3, /device:TPU:0, one launch (start us, length us, event | category | flops | bytes accessed | tf_op | source)
XLA Modules:
  0.0 103.4 jit_solution(2657240438698104675)
XLA Ops:
  0.0 0.0 copy-start.1
  0.7 0.7 pad_add_fusion.meta_ref
  1.3 28.7 %gather.1 = bf16[12,512,256]{2,1,0:T(8,128)(2,1)} custom-call(bf16[512,256]{1,0:T(8,128)(2,1)} %f_ref.1), custom_call_target="tpu_custom_call" | custom-call | tf_op jit(solution)/shard_map/gather/pallas_call | solution.py:502
  30.1 0.0 copy-done.1
  30.1 0.1 copy.7
  30.2 0.7 reshape.21.coord_ref
  30.9 0.0 copy-start
  30.9 12.1 %tile_pass.1 = (s16[16,256,256]{2,1,0:T(8,128)(2,1)}, s16[8,256,256]{2,1,0:T(8,128)(2,1)}, f32[16,1,256]{2,1,0:T(1,128)}, f32[8,1,256]{2,1,0:T(1,128)}) custom-call(s32[192]{0:T(256)} %reshape.21.coord_ref, s32[4]{0:T(128)} %pad_add_fusion.meta_ref, bf16[96,256,256]{2,1,0:T(8,128)(2,1)} %bitcast.13, bf16[24,256,256]{2,1,0:T(8,128)(2,1)} %bitcast.14), custom_call_target="tpu_custom_call" | custom-call | tf_op jit(solution)/shard_map/tile_pass/pallas_call | solution.py:522
  43.0 0.0 copy-done
  43.0 0.9 copy.8.owner_sub
  43.9 57.6 %solve.1 = f32[512,256]{1,0:T(8,128)} custom-call(s16[8,512,256]{2,1,0:T(8,128)(2,1)} %bitcast.15, s16[4,512,256]{2,1,0:T(8,128)(2,1)} %bitcast.16, f32[16,1,256]{2,1,0:T(1,128)} %get-tuple-element.11.srow_ref, f32[8,1,256]{2,1,0:T(1,128)} %get-tuple-element.12.scol_ref, s32[1,512]{1,0:T(1,128)} %bitcast.17, s32[512,1]{1,0:T(8,128)} %copy.8.owner_sub, ...), custom_call_target="tpu_custom_call" | custom-call | tf_op jit(solution)/shard_map/solve/pallas_call | solution.py:562
  101.5 1.9 %copy.11 = f32[512,256]{1,0:T(8,128)} copy(f32[512,256]{1,0:T(8,128)} %solve.1) | data formatting | bytes 1048576
Async XLA Ops:
  0.0 30.1 %copy-start.1 = (s32[1,1,96,2]{2,3,1,0:T(2,128)S(1)}, s32[1,1,96,2]{2,3,1,0:T(2,128)}, u32[]{:S(2)}) copy-start(s32[1,1,96,2]{2,3,1,0:T(2,128)} %param.7) | copy-start | bytes 2308
  30.9 12.1 %copy-start = (s32[512]{0:T(512)S(1)}, s32[512]{0:T(512)}, u32[]{:S(2)}) copy-start(s32[512]{0:T(512)} %param.10) | copy-start | bytes 6148

commit v4 on v3

--- a/solution.py
+++ b/solution.py
@@ -340,10 +340,10 @@
                     copy.start()
 
     for n in range(max(chips - 1, PARTS)):
+        if n < PARTS:
+            relay(n)
         if n < chips - 1:
             pair_sum(n + 1)
-        if n < PARTS:
-            relay(n)
 
     def add(coded_ref, scales_ref, s, at=None):
         for t in range(tpd):

time: 105 us -> 104 us (level)
  Pallas kernels: 98.5 us -> 96.8 us
    pallas_call x1, Pallas kernels: 57.6 us -> 55.9 us  [per_device(): pl.pallas_call(functools.partial(solve_kernel, n_row, n_col, pad, tile_di...]
where the time goes in v4:
time: 104 us; the launch traced here: 102 us
  Pallas kernels  96.8 us (93%)
  local copies, waits for them, and re-layouts  3.54 us (3%)
    pallas_call x1, Pallas kernels, per_device(): pl.pallas_call(functools.partial(solve_kernel, n_row, n_col, pad, tile_di...  55.9 us
    pallas_call x1, Pallas kernels, per_device(): pl.pallas_call(functools.partial(gather_kernel, n_row, n_col), out_shape=...  28.7 us
    pallas_call x1, Pallas kernels, per_device(): pl.pallas_call(functools.partial(tile_kernel, per_step), out_shape=(jax.S...  12.1 us

profile of v4, /device:TPU:0, one launch (start us, length us, event | category | flops | bytes accessed | tf_op | source)
XLA Modules:
  0.0 101.7 jit_solution(16558244555909983204)
XLA Ops:
  0.0 0.0 copy-start.1
  0.7 0.7 pad_add_fusion.meta_ref
  1.3 28.7 %gather.1 = bf16[12,512,256]{2,1,0:T(8,128)(2,1)} custom-call(bf16[512,256]{1,0:T(8,128)(2,1)} %f_ref.1), custom_call_target="tpu_custom_call" | custom-call | tf_op jit(solution)/shard_map/gather/pallas_call | solution.py:502
  30.1 0.0 copy-done.1
  30.1 0.1 copy.7
  30.2 0.7 reshape.21.coord_ref
  30.9 0.0 copy-start
  30.9 12.1 %tile_pass.1 = (s16[16,256,256]{2,1,0:T(8,128)(2,1)}, s16[8,256,256]{2,1,0:T(8,128)(2,1)}, f32[16,1,256]{2,1,0:T(1,128)}, f32[8,1,256]{2,1,0:T(1,128)}) custom-call(s32[192]{0:T(256)} %reshape.21.coord_ref, s32[4]{0:T(128)} %pad_add_fusion.meta_ref, bf16[96,256,256]{2,1,0:T(8,128)(2,1)} %bitcast.13, bf16[24,256,256]{2,1,0:T(8,128)(2,1)} %bitcast.14), custom_call_target="tpu_custom_call" | custom-call | tf_op jit(solution)/shard_map/tile_pass/pallas_call | solution.py:522
  43.0 0.0 copy-done
  43.0 0.9 copy.8.owner_sub
  43.9 55.9 %solve.1 = f32[512,256]{1,0:T(8,128)} custom-call(s16[8,512,256]{2,1,0:T(8,128)(2,1)} %bitcast.15, s16[4,512,256]{2,1,0:T(8,128)(2,1)} %bitcast.16, f32[16,1,256]{2,1,0:T(1,128)} %get-tuple-element.11.srow_ref, f32[8,1,256]{2,1,0:T(1,128)} %get-tuple-element.12.scol_ref, s32[1,512]{1,0:T(1,128)} %bitcast.17, s32[512,1]{1,0:T(8,128)} %copy.8.owner_sub, ...), custom_call_target="tpu_custom_call" | custom-call | tf_op jit(solution)/shard_map/solve/pallas_call | solution.py:562
  99.8 1.9 %copy.11 = f32[512,256]{1,0:T(8,128)} copy(f32[512,256]{1,0:T(8,128)} %solve.1) | data formatting | bytes 1048576
Async XLA Ops:
  0.0 30.1 %copy-start.1 = (s32[1,1,96,2]{2,3,1,0:T(2,128)S(1)}, s32[1,1,96,2]{2,3,1,0:T(2,128)}, u32[]{:S(2)}) copy-start(s32[1,1,96,2]{2,3,1,0:T(2,128)} %param.7) | copy-start | bytes 2308
  30.9 12.1 %copy-start = (s32[512]{0:T(512)S(1)}, s32[512]{0:T(512)}, u32[]{:S(2)}) copy-start(s32[512]{0:T(512)} %param.10) | copy-start | bytes 6148
